TPU v7x, 128 devices: a whole 4x4x4 slice. The times are simulated.
128 devices in a mesh: dp: 2 (over core), expert: 8 (over x_lo, z), etp: 8 (over x_hi, y).
Axes of the slice: x: 4 (x_hi: 2, x_lo: 2; x = x_hi * 2 + x_lo), y: 4, z: 4, core: 2. Of those that a mesh axis runs over, the one named last changes fastest.
Arguments:
- grad_out: bfloat16 [16384, 3072], P(('dp', 'expert', 'etp')), may hold values from -6 to 6
- expert_ids: int32 [16384, 2], P(('dp', 'expert', 'etp')), may hold values from 0 to 7, all different within a row; in each aligned block of 128 rows (0 to 127, 128 to 255, ...) at most 36 rows name the same one
- gate_probs: bfloat16 [16384, 2], P(('dp', 'expert', 'etp')), may hold values from 0.099609375 to 0.8984375
- keep_mask: int32 [16384, 2], P(('dp', 'expert', 'etp')), may hold values 0 or 1
- pre_gate: bfloat16 [8, 4608, 8192], P('expert', 'dp', 'etp'), may hold values from -4 to 4
- pre_up: bfloat16 [8, 4608, 8192], P('expert', 'dp', 'etp'), may hold values from -4 to 4
- w_down: bfloat16 [8, 8192, 3072], P('expert', 'etp', 'dp'), may hold values from -0.0625 to 0.0625
Outputs:
- grad_pre_gate: bfloat16 [8, 4608, 8192], P('expert', 'dp', 'etp')
- grad_pre_up: bfloat16 [8, 4608, 8192], P('expert', 'dp', 'etp')
- grad_w_down: bfloat16 [8, 8192, 3072], P('expert', 'etp', 'dp')
- grad_gate_probs: float32 [16384, 2], P(('dp', 'expert', 'etp'))
Inputs may be any that keep to these rules, and one draw needn't show every extreme that they name: `expert_ids`: the two experts of a token differ. Among the 128 tokens of one device no expert is chosen more than 36 times, and on some devices one expert is chosen exactly 36 times.
All inputs are finite; a program needn't handle non-finite values. No bound on the sum of `keep_mask` on one device may be relied on, other than what follows from the above.
Results may differ from a plain program's by a relative error of at most 0.0058.
Values may be sent and summed in bfloat16 or wider, within the bound.
No kernel may reach another device: no remote copies, remote signals or barrier semaphores. Data moves between devices by JAX's collectives and lax.ppermute only.
A program may use at most 192 MiB of HBM per device.

v0:
```python
import jax
import jax.numpy as jnp
from jax import lax
from jax.sharding import PartitionSpec as P


def activation_grads(gate_pre, up_pre, back_full, gate_column):
    pre_gate = gate_pre.astype(jnp.float32)
    pre_up = up_pre.astype(jnp.float32)
    sigmoid_gate = jax.nn.sigmoid(pre_gate)
    swish_gate = pre_gate * sigmoid_gate
    product = swish_gate * pre_up
    hidden_act = product.astype(jnp.bfloat16)
    upstream = gate_column.astype(jnp.float32) * back_full
    grad_gate = (
        upstream * pre_up * (sigmoid_gate * (1.0 + pre_gate * (1.0 - sigmoid_gate)))
    ).astype(jnp.bfloat16)
    grad_upper = (upstream * swish_gate).astype(jnp.bfloat16)
    gate_term = jnp.sum(product * back_full, axis=1)
    return (hidden_act, grad_gate, grad_upper, gate_term)


def contract_rows(left, right):
    return lax.dot_general(
        left, right, (((0,), (0,)), ((), ())), preferred_element_type=jnp.float32
    )


def contract_cols(left, right):
    return lax.dot_general(
        left, right, (((1,), (1,)), ((), ())), preferred_element_type=jnp.float32
    )


def local(grad_out, expert_ids, gate_probs, keep_mask, pre_gate, pre_up, w_down):
    experts = lax.axis_size("expert")
    replicas = lax.axis_size("dp")
    sharers = lax.axis_size("etp")
    tok_count = grad_out.shape[0]
    model_width = grad_out.shape[1]
    half_width = model_width // replicas
    local_rows = pre_gate.shape[1]
    capacity = local_rows // (experts * sharers)
    flat_ids = expert_ids.reshape(-1)
    onehot = (flat_ids[:, None] == jnp.arange(experts, dtype=jnp.int32)[None, :]).astype(jnp.int32)
    before = jnp.cumsum(onehot, axis=0) - onehot
    slot_index = jnp.sum(before * onehot, axis=1)
    target = flat_ids * capacity + slot_index
    kept_gate = (gate_probs * keep_mask.astype(jnp.bfloat16)).reshape(-1)
    send_grads = (
        jnp.zeros((experts * capacity, model_width), jnp.bfloat16)
        .at[target]
        .set(jnp.repeat(grad_out, 2, axis=0))
    )
    send_gates = jnp.zeros((experts * capacity,), jnp.bfloat16).at[target].set(kept_gate)
    gate_local = pre_gate[0]
    up_local = pre_up[0]
    down_local = w_down[0]
    gate_copies = jnp.broadcast_to(send_gates[:, None], (experts * capacity, replicas))
    arrived_grads, arrived_gates = (
        lax.all_to_all(
            lax.all_to_all(
                send_grads.reshape(1, experts, capacity, model_width),
                "dp",
                split_axis=3,
                concat_axis=0,
                tiled=True,
            ),
            "expert",
            split_axis=1,
            concat_axis=1,
            tiled=True,
        ),
        lax.all_to_all(
            lax.all_to_all(
                gate_copies.reshape(1, experts, capacity, replicas),
                "dp",
                split_axis=3,
                concat_axis=0,
                tiled=True,
            ),
            "expert",
            split_axis=1,
            concat_axis=1,
            tiled=True,
        ),
    )
    all_grads, all_gates = (
        lax.all_gather(arrived_grads, "etp", axis=2, tiled=True),
        lax.all_gather(arrived_gates, "etp", axis=2, tiled=True),
    )
    grad_rows = all_grads.reshape(-1, half_width)
    gate_rows = all_gates.reshape(-1, 1)
    back_part = contract_cols(grad_rows, down_local)
    back_share = lax.psum_scatter(back_part, "dp", scatter_dimension=0, tiled=True)
    gate_share = lax.dynamic_slice_in_dim(
        gate_rows, lax.axis_index("dp") * local_rows, local_rows, 0
    )
    hidden_act, grad_gate, grad_upper, gate_term = activation_grads(
        gate_local, up_local, back_share, gate_share
    )
    hidden_all = lax.all_gather(hidden_act, "dp", axis=0, tiled=True)
    scaled = (gate_rows.astype(jnp.float32) * grad_rows.astype(jnp.float32)).astype(jnp.bfloat16)
    wgrad_down = contract_rows(hidden_all, scaled).astype(jnp.bfloat16)
    term_sums = lax.psum_scatter(
        gate_term.reshape(experts, sharers * capacity), "etp", scatter_dimension=1, tiled=True
    )
    returned = lax.all_to_all(term_sums, "expert", split_axis=0, concat_axis=0, tiled=True).reshape(
        -1
    )
    picked = jnp.take(returned, target, axis=0).reshape(tok_count, 2)
    grad_gate_probs = keep_mask.astype(jnp.float32) * picked
    return (grad_gate[None], grad_upper[None], wgrad_down[None], grad_gate_probs)


def solution(mesh):
    in_specs = (
        P(("dp", "expert", "etp"), None),
        P(("dp", "expert", "etp"), None),
        P(("dp", "expert", "etp"), None),
        P(("dp", "expert", "etp"), None),
        P("expert", "dp", "etp"),
        P("expert", "dp", "etp"),
        P("expert", "etp", "dp"),
    )
    out_specs = (
        P("expert", "dp", "etp"),
        P("expert", "dp", "etp"),
        P("expert", "etp", "dp"),
        P(("dp", "expert", "etp"), None),
    )
    return jax.shard_map(local, mesh=mesh, in_specs=in_specs, out_specs=out_specs, check_vma=False)
```

profile of v0, /device:TPU:0, one launch (start us, length us, event | category | flops | bytes accessed | tf_op | source)
XLA Modules:
  0.0 466.4 jit_solution(6089472426875288177)
XLA Ops:
  7.2 0.9 copy.35
  9.5 3.1 broadcast_in_dim.39
  12.5 4.6 reshape.140
  17.3 5.3 %scatter_custom_fusion.1 = bf16[288,3072]{1,0:T(8,128)(2,1)} fusion(s32[256]{0:T(256)S(1)} %bitcast.77, bf16[256,3072]{1,0:T(8,128)(2,1)} %reshape.140, bf16[]{:T(256)} %constant.12.clone.1), kind=kCustom, calls=%fused_computation.27 | custom fusion | bytes 1769984 | tf_op jit(solution)/shard_map/scatter | solution.py:53
  22.5 2.6 reshape.112
  25.1 7.6 %copy.42 = bf16[1,8,36,3072]{2,1,0,3:T(8,128)(2,1)} copy(bf16[1,8,36,3072]{3,2,1,0:T(8,128)(2,1)} %reshape.112) | data formatting | bytes 3538944 | tf_op jit(solution)/shard_map/reshape | solution.py:63
  32.7 18.6 %reshape.164 = bf16[2,2,221184]{2,1,0:T(2,128)(2,1)} reshape(bf16[3072,1,8,36]{3,2,1,0:T(8,128)(2,1)} %bitcast.71) | data formatting | bytes 3538944
  51.3 8.7 %all_to_all.55 = bf16[2,2,221184]{2,1,0:T(2,128)(2,1)} all-to-all(bf16[2,2,221184]{2,1,0:T(2,128)(2,1)} %reshape.164), channel_id=1, replica_groups=mesh['dp'=2,'expert'=8,'etp'=8] {'dp'}, dimensions={0} | all-to-all | bytes 3538944 | tf_op jit(solution)/shard_map/all_to_all | solution.py:62
  60.0 19.9 %reshape.165 = bf16[3072,1,8,36]{3,2,1,0:T(8,128)(2,1)} reshape(bf16[2,2,221184]{2,1,0:T(2,128)(2,1)} %all_to_all.55) | data formatting | bytes 3538944
  79.9 10.6 %copy.52 = bf16[1,8,36,2,1536]{4,3,2,1,0:T(2,128)(2,1)} copy(bf16[1,8,36,2,1536]{2,1,4,3,0:T(8,128)(2,1)} %bitcast.72) | data formatting | bytes 3538944 | tf_op jit(solution)/shard_map/all_to_all | solution.py:62
  90.5 30.0 %all_to_all.56 = bf16[2,8,36,1536]{3,0,2,1:T(2,128)(2,1)S(1)} all-to-all(bf16[2,8,36,1536]{3,0,2,1:T(2,128)(2,1)} %bitcast.75), channel_id=1, replica_groups=mesh['dp'=2,'expert'=8,'etp'=8] {'expert'}, dimensions={1} | all-to-all | bytes 3538944 | tf_op jit(solution)/shard_map/all_to_all | solution.py:61
  120.6 1.7 copy.45
  122.5 157.9 %all-gather.3.cloned.1.call-done = bf16[2,8,288,1536]{3,1,0,2:T(8,128)(2,1)} async-done(((bf16[2,8,36,1536]{3,1,0,2:T(8,128)(2,1)}), bf16[2,8,288,1536]{3,1,0,2:T(8,128)(2,1)}) %all-gather.3.cloned.1.call-update) | async-done | bytes 14155792 | tf_op jit(solution)/shard_map/all_gather | solution.py:89
  280.5 10.3 %copy.46 = bf16[2,8,288,1536]{3,2,1,0:T(8,128)(2,1)S(1)} copy(bf16[2,8,288,1536]{3,1,0,2:T(8,128)(2,1)} %all-gather.3.cloned.1.call-done) | data formatting | bytes 28311552 | tf_op jit(solution)/shard_map/all_gather | solution.py:89
  290.8 5.0 %copy-done.2 = bf16[2,8,288,1536]{3,2,1,0:T(8,128)(2,1)} copy-done((bf16[2,8,288,1536]{3,2,1,0:T(8,128)(2,1)}, bf16[2,8,288,1536]{3,2,1,0:T(8,128)(2,1)S(1)}, u32[]{:S(2)}) %copy-start.2) | copy-done | bytes 14155800
  295.8 19.2 %fusion.14 = f32[4608,1024]{1,0:T(8,128)} fusion(bf16[4608,1536]{1,0:T(8,128)(2,1)S(1)} %bitcast.73, bf16[1,1024,1536]{2,1,0:T(8,128)(2,1)S(1)} %copy-done), kind=kOutput, calls=%fused_computation.25 | convolution fusion | flops 14495514624 | bytes 36175872 | tf_op jit(solution)/shard_map/dot_general | solution.py:30
  315.0 0.7 copy-done.3
  315.9 2.2 scatter_custom_fusion
  318.3 3.7 all_to_all.57
  322.0 0.6 copy.39
  322.6 4.4 all-to-all-start.1
  327.1 6.0 %all-to-all-done.1 = bf16[2,8,36,1]{2,0,3,1:T(2,128)(2,1)S(1)} async-done(((bf16[2,8,36,1]{2,0,3,1:T(2,128)(2,1)}), bf16[2,8,36,1]{2,0,3,1:T(2,128)(2,1)S(1)}, u32[]{:S(2)}, u32[]{:S(2)}) %all-to-all-start.1) | async-done | bytes 1184 | tf_op jit(solution)/shard_map/all_to_all | solution.py:74
  333.3 34.2 %all_gather.9 = bf16[2,8,288,1]{1,0,3,2:T(2,128)(2,1)S(1)} all-gather(bf16[2,8,36,1]{1,0,3,2:T(2,128)(2,1)S(1)} %copy.40), channel_id=1, replica_groups=mesh['dp'=2,'expert'=8,'etp'=8] {'etp'}, dimensions={2}, use_global_device_ids=true | all-gather | bytes 10368 | tf_op jit(solution)/shard_map/all_gather | solution.py:90
  367.8 15.8 %multiply_reduce_fusion = (f32[2304]{0:T(1024)S(1)}, bf16[1,2304,1024]{2,1,0:T(8,128)(2,1)}, bf16[1,2304,1024]{2,1,0:T(8,128)(2,1)}, bf16[2304,1024]{1,0:T(8,128)(2,1)}) fusion(f32[2304,1024]{1,0:T(8,128)} %reduce-scatter.3.cloned.1.call-done, bf16[1,2304,1024]{2,1,0:T(8,128)(2,1)} %param.12, bf16[1,2304,1024]{2,1,0:T(8,128)(2,1)} %param.11, ...), kind=kLoop, calls=%fused_computation.18 | loop fusion | flops 47183616 | bytes 33048576 | tf_op jit(solution)/shard_map/reduce_sum | solution.py:19
  385.0 38.8 %all-reduce = f32[8,288]{1,0:T(8,128)S(1)} all-reduce(f32[8,288]{1,0:T(8,128)S(1)} %reshape.114), channel_id=3, replica_groups=mesh['dp'=2,'expert'=8,'etp'=8] {'etp'}, use_global_device_ids=true, to_apply=%region_7.8.clone | all-reduce | flops 2304 | bytes 18432
  423.8 0.7 constant_dynamic-slice_fusion
  424.5 3.5 all-to-all-start.4
  428.5 5.5 %all-to-all-done.4 = f32[8,1,36]{2,1,0:T(1,128)S(1)} async-done(((f32[8,1,36]{2,1,0:T(1,128)}), f32[8,1,36]{2,1,0:T(1,128)S(1)}, u32[]{:S(2)}, u32[]{:S(2)}) %all-to-all-start.4) | async-done | bytes 1184 | tf_op jit(solution)/shard_map/all_to_all | solution.py:108
  434.5 0.7 reduce.7
  435.3 1.9 gather_fusion
  437.4 0.6 copy.50
  438.0 21.6 %fusion.13 = bf16[1,1024,1536]{2,1,0:T(8,128)(2,1)} fusion(bf16[4608,1024]{1,0:T(8,128)(2,1)} %all-gather.5.cloned.1.call-done, bf16[4608,1536]{1,0:T(8,128)(2,1)} %bitcast.74, f32[4608]{0:T(1024)S(1)} %reshape.119), kind=kOutput, calls=%fused_computation.24 | convolution fusion | flops 14518321152 | bytes 26757120 | tf_op jit(solution)/shard_map/dot_general | solution.py:24
  (53 shorter events, 4.6 us)
Async XLA Ops:
  7.2 288.6 %copy-start = (bf16[1,1024,1536]{2,1,0:T(8,128)(2,1)S(1)}, bf16[1,1024,1536]{2,1,0:T(8,128)(2,1)}, u32[]{:S(2)}) copy-start(bf16[1,1024,1536]{2,1,0:T(8,128)(2,1)} %param.13) | copy-start | bytes 9437188
  7.2 273.3 %all-gather.3.cloned.1.call-start = ((), (), s32[]{:S(2)}) async-start(), calls=%async_computation.6 | async-start | bytes 15925248 | tf_op jit(solution)/shard_map/all_gather | solution.py:89
  122.3 245.5 %reduce-scatter.3.cloned.1.call-start = ((), (), s32[]{:S(2)}) async-start(), calls=%async_computation.7 | async-start | bytes 28311552 | tf_op jit(solution)/shard_map/reduce_scatter | solution.py:95
  290.8 5.0 %copy-start.2 = (bf16[2,8,288,1536]{3,2,1,0:T(8,128)(2,1)}, bf16[2,8,288,1536]{3,2,1,0:T(8,128)(2,1)S(1)}, u32[]{:S(2)}) copy-start(bf16[2,8,288,1536]{3,2,1,0:T(8,128)(2,1)S(1)} %copy.46) | copy-start | bytes 42467332
  314.9 0.7 copy-start.3
  314.9 0.7 copy-start.4
  322.6 10.5 %all-to-all-start.1 = ((bf16[2,8,36,1]{2,0,3,1:T(2,128)(2,1)}), bf16[2,8,36,1]{2,0,3,1:T(2,128)(2,1)S(1)}, u32[]{:S(2)}, u32[]{:S(2)}) async-start(bf16[2,8,36,1]{2,0,3,1:T(2,128)(2,1)} %copy.39), calls=%async_computation.1 | async-start | bytes 8192 | tf_op jit(solution)/shard_map/all_to_all | solution.py:74
  327.1 111.0 %all-gather.5.cloned.1.call-start = ((), (), s32[]{:S(2)}) async-start(), calls=%async_computation.8 | async-start | bytes 14155776 | tf_op jit(solution)/shard_map/all_gather | solution.py:102
  367.8 15.9 %copy-start.5 = (u32[128]{0:T(128)S(1)}, u32[128]{0:T(128)}, u32[]{:S(2)}) copy-start(u32[128]{0:T(128)} %constant.47) | copy-start | bytes 1540
  424.5 9.5 %all-to-all-start.4 = ((f32[8,1,36]{2,1,0:T(1,128)}), f32[8,1,36]{2,1,0:T(1,128)S(1)}, u32[]{:S(2)}, u32[]{:S(2)}) async-start(f32[8,1,36]{2,1,0:T(1,128)} %bitcast.21), calls=%async_computation.5 | async-start | bytes 8192 | tf_op jit(solution)/shard_map/all_to_all | solution.py:108
  438.0 21.6 %copy-start.1 = (bf16[1,1024,1536]{2,1,0:T(8,128)(2,1)S(1)}, bf16[1,1024,1536]{2,1,0:T(8,128)(2,1)}, u32[]{:S(2)}) copy-start(bf16[1,1024,1536]{2,1,0:T(8,128)(2,1)} %param.13) | copy-start | bytes 9437188
Sparse Core Ops, SparseCore 0:
  122.4 157.9 all-gather.2
  315.1 28.9 reduce-scatter.2
  383.8 20.6 all-gather.4
where the time goes:
time: 472 us; the launch traced here: 466 us
  waiting for transfers between devices  170 us (36%)
  blocking collectives  115 us (24%)
  local copies, waits for them, and re-layouts  100 us (21%)
  matrix products  40.8 us (9%)
  other arithmetic  17.3 us (4%)
  between operations  14.8 us (3%)
  starting transfers between devices  8.24 us (2%)
    all_gather x1, waiting for transfers between devices, local(): lax.all_gather(arrived_grads, 'etp', axis=2, tiled=True)  158 us
    unnamed x21, local copies, waits for them, and re-layouts  47.2 us
    unnamed x1, blocking collectives  38.8 us
    all_gather x1, blocking collectives, local(): lax.all_gather(arrived_gates, 'etp', axis=2, tiled=True)  34.2 us
    all_to_all x1, blocking collectives, local(): lax.all_to_all(lax.all_to_all(send_grads.reshape(1, experts, capacity, mo...  30 us
    dot_general x1, matrix products, contract_rows(): lax.dot_general(left, right, (((0,), (0,)), ((), ())), preferred_element_...  21.6 us
    dot_general x1, matrix products, contract_cols(): lax.dot_general(left, right, (((1,), (1,)), ((), ())), preferred_element_...  19.2 us
    reduce_sum x1, other arithmetic, activation_grads(): gate_term = jnp.sum(product * back_full, axis=1)  15.8 us
  transfers between devices with their start and end apart: 5, of which 3 were waited for; matrix products, arithmetic and copies ran while one was open for 2% of the time, Pallas kernels for 0%

commit v1 on v0

v1 whole, which is shorter than its diff:
```python
import functools

import jax
import jax.numpy as jnp
from jax import lax
from jax.experimental import pallas as pl
from jax.experimental.pallas import tpu as pltpu
from jax.sharding import PartitionSpec as P

AXES = ("dp", "expert", "etp")
EXPERTS = 8
CAP = 36
TOK = 128
D = 3072
HALF = 1536
FF = 1024
ROWS = 2304
PAIR = 2 * CAP
UNIT = 4 * CAP
FT = 256
VMEM = 56 * 1024 * 1024


def position(flat):
    dp, rest = divmod(flat, 64)
    expert, etp = divmod(rest, 8)
    x_lo, z = divmod(expert, 4)
    x_hi, y = divmod(etp, 4)
    return dp, x_hi * 2 + x_lo, y, z


def flat_of(dp, x, y, z):
    return dp * 64 + ((x % 2) * 4 + z) * 8 + (x // 2) * 4 + y


def move(array, step):
    pairs = []
    for source in range(128):
        dp, x, y, z = position(source)
        pairs.append((source, flat_of(*step(dp, x, y, z))))
    return lax.ppermute(array, AXES, pairs)


def along_x(k):
    return lambda dp, x, y, z: (dp, (x + k) % 4, y, z)


def along_z(k):
    return lambda dp, x, y, z: (dp, x, y, (z + k) % 4)


def turned(dp, y, change):
    return (change((y - dp) % 4) + dp) % 4


def near_pair(dp, x, y, z):
    return dp, x, turned(dp, y, lambda v: v ^ 1), z


def far_pair(dp, x, y, z):
    return dp, x, turned(dp, y, lambda v: 3 - v), z


def other_core(dp, x, y, z):
    return 1 - dp, x, y, z


def slot_lines(meta):
    names = lax.broadcasted_iota(jnp.int32, (EXPERTS, TOK), 0).astype(jnp.float32)
    first = (names == meta[0:1, :]).astype(jnp.float32)
    second = (names == meta[1:2, :]).astype(jnp.float32)
    row = lax.broadcasted_iota(jnp.int32, (TOK, TOK), 0)
    col = lax.broadcasted_iota(jnp.int32, (TOK, TOK), 1)
    earlier = (row < col).astype(jnp.bfloat16)
    before = jnp.dot(
        (first + second).astype(jnp.bfloat16), earlier, preferred_element_type=jnp.float32
    )
    return (
        jnp.sum(before * first, axis=0, keepdims=True),
        jnp.sum(before * second, axis=0, keepdims=True),
    )


def slots_kernel(sp, own_meta, par_meta, own_x, par_x, s0, s1, s2, s3, slot_out):
    z, x_lo, odd = sp[0], sp[1], sp[2]
    own_slots = slot_lines(own_meta[...])
    par_slots = slot_lines(par_meta[...])
    slot_out[...] = jnp.concatenate(
        [own_slots[0], own_slots[1], jnp.zeros((6, TOK), jnp.float32)], axis=0
    )
    row = lax.broadcasted_iota(jnp.int32, (UNIT, 1), 0)
    other = row >= PAIR
    within = jnp.where(other, row - PAIR, row)
    late = (within >= CAP).astype(jnp.int32)
    slot = jnp.where(within >= CAP, within - CAP, within).astype(jnp.float32)
    lo = jnp.where(other, 1 - x_lo, x_lo)
    for k, out in enumerate((s0, s1, s2, s3)):
        z_to = lax.rem(z + k, 4)
        expert = (lo * 4 + z_to).astype(jnp.float32)
        total = jnp.zeros((UNIT, own_x.shape[1]), jnp.float32)
        for mine, meta, slots, x in (
            (True, own_meta, own_slots, own_x),
            (False, par_meta, par_slots, par_x),
        ):
            here = late == (odd if mine else 1 - odd)
            pick = jnp.zeros((UNIT, TOK), jnp.float32)
            for j in range(2):
                hit = (meta[j : j + 1, :] == expert) & (slots[j] == slot) & here
                pick = pick + jnp.where(hit, meta[2 + j : 3 + j, :], 0.0)
            total = total + jnp.dot(
                pick.astype(jnp.bfloat16), x[...], preferred_element_type=jnp.float32
            )
        out[...] = total.astype(jnp.bfloat16)


def build_slots(sp, own_meta, par_meta, own_x, par_x):
    tile = 1024
    whole = pl.BlockSpec((8, TOK), lambda i, sp: (0, 0))
    tokens = pl.BlockSpec((TOK, tile), lambda i, sp: (0, i))
    return pl.pallas_call(
        slots_kernel,
        grid_spec=pltpu.PrefetchScalarGridSpec(
            num_scalar_prefetch=1,
            grid=(D // tile,),
            in_specs=[whole, whole, tokens, tokens],
            out_specs=[pl.BlockSpec((UNIT, tile), lambda i, sp: (0, i))] * 4 + [whole],
        ),
        out_shape=[jax.ShapeDtypeStruct((UNIT, D), jnp.bfloat16)] * 4
        + [jax.ShapeDtypeStruct((8, TOK), jnp.float32)],
        cost_estimate=pl.CostEstimate(
            flops=2 * 4 * UNIT * 2 * TOK * D, bytes_accessed=6_000_000, transcendentals=0
        ),
        compiler_params=pltpu.CompilerParams(vmem_limit_bytes=VMEM),
    )(sp, own_meta, par_meta, own_x, par_x)


def chunk_kernel(first, last, sp, *refs):
    own_y, par_y, own_w, oth_w, gate, up = refs[:6]
    refs = refs[6:]
    if not first:
        sums_in, refs = refs[:2], refs[5:]
    grad_gate, grad_up, term, sums = refs[0], refs[1], refs[2], refs[3:5]
    back_s, hid_s, term_s = refs[5:]
    f = pl.program_id(0)
    mine = pl.ds(pl.multiple_of(sp[11], 128), HALF)
    others = pl.ds(pl.multiple_of(sp[12], 128), HALF)
    nt = (((1,), (1,)), ((), ()))
    tn = (((0,), (0,)), ((), ()))
    for side, y in enumerate((own_y, par_y)):
        back = lax.dot_general(y[:, mine], own_w[...], nt, preferred_element_type=jnp.float32)
        back = back + lax.dot_general(
            y[:, others], oth_w[...], nt, preferred_element_type=jnp.float32
        )
        for j in range(4):
            start = pl.multiple_of(sp[1 + side * 4 + j], 8)
            back_s[pl.ds(start, PAIR), :] = back[j * PAIR : (j + 1) * PAIR]
    for unit in range(4):
        rows = pl.ds(unit * UNIT, UNIT)
        upstream = pltpu.roll(back_s[rows, :], sp[9], 0)
        half, part = unit // 2, pl.ds((unit % 2) * UNIT, UNIT)
        a = gate[half, 0, part, :].astype(jnp.float32)
        b = up[half, 0, part, :].astype(jnp.float32)
        s = jax.nn.sigmoid(a)
        swish = a * s
        product = swish * b
        grad_gate[half, 0, part, :] = (upstream * b * (s * (1.0 + a * (1.0 - s)))).astype(
            jnp.bfloat16
        )
        grad_up[half, 0, part, :] = (upstream * swish).astype(jnp.bfloat16)
        term_here = product * upstream
        term_here = term_here[:, 0:128] + term_here[:, 128:256]

        @pl.when(f == 0)
        def _():
            term_s[rows, :] = term_here

        @pl.when(f > 0)
        def _():
            term_s[rows, :] += term_here

        hid_s[rows, :] = pltpu.roll(product, sp[10], 0)

    @pl.when(f == pl.num_programs(0) - 1)
    def _():
        for half in range(2):
            term[half, 0, :, :] = jnp.sum(
                term_s[pl.ds(half * 2 * UNIT, 2 * UNIT), :], axis=1, keepdims=True
            )

    total = [None, None]
    for side, y in enumerate((own_y, par_y)):
        hidden = jnp.concatenate(
            [
                hid_s[pl.ds(pl.multiple_of(sp[1 + side * 4 + j], 8), PAIR), :]
                for j in range(4)
            ],
            axis=0,
        ).astype(jnp.bfloat16)
        for i, cols in enumerate((mine, others)):
            part = lax.dot_general(hidden, y[:, cols], tn, preferred_element_type=jnp.float32)
            total[i] = part if side == 0 else total[i] + part
    for i in range(2):
        if not first:
            total[i] = total[i] + sums_in[i][...]
        sums[i][...] = total[i].astype(sums[i].dtype)


def run_chunk(first, last, sp, own_y, par_y, own_w, oth_w, gate, up, sums, carried):
    pre = pl.BlockSpec((2, 1, 2 * UNIT, FT), lambda f, sp: (0, sp[0], 0, f))
    rows = pl.BlockSpec((4 * PAIR, D), lambda f, sp: (0, 0))
    weight = pl.BlockSpec((FT, HALF), lambda f, sp: (f, 0))
    in_specs = [rows, rows, weight, weight, pre, pre]
    operands = [own_y, par_y, own_w, oth_w, gate, up]
    aliases = {}
    if not first:
        in_specs += [weight, weight] + [pl.BlockSpec(memory_space=pl.ANY)] * 3
        operands += list(sums) + list(carried)
        aliases = {9: 0, 10: 1, 11: 2}
    shape = jax.ShapeDtypeStruct
    other_type = jnp.bfloat16 if last else jnp.float32
    out = pl.pallas_call(
        functools.partial(chunk_kernel, first, last),
        grid_spec=pltpu.PrefetchScalarGridSpec(
            num_scalar_prefetch=1,
            grid=(FF // FT,),
            in_specs=in_specs,
            out_specs=[
                pre,
                pre,
                pl.BlockSpec((2, 1, 2 * UNIT, 1), lambda f, sp: (0, sp[0], 0, 0)),
                weight,
                weight,
            ],
            scratch_shapes=[
                pltpu.VMEM((4 * UNIT, FT), jnp.float32),
                pltpu.VMEM((4 * UNIT, FT), jnp.float32),
                pltpu.VMEM((4 * UNIT, 128), jnp.float32),
            ],
        ),
        out_shape=[
            shape((2, 4, 2 * UNIT, FF), jnp.bfloat16),
            shape((2, 4, 2 * UNIT, FF), jnp.bfloat16),
            shape((2, 4, 2 * UNIT, 1), jnp.float32),
            shape((FF, HALF), jnp.float32),
            shape((FF, HALF), other_type),
        ],
        input_output_aliases=aliases,
        cost_estimate=pl.CostEstimate(
            flops=4 * 4 * UNIT * D * FF,
            bytes_accessed=30_000_000,
            transcendentals=4 * UNIT * FF,
        ),
        compiler_params=pltpu.CompilerParams(vmem_limit_bytes=VMEM),
    )(sp, *operands)
    return out[:3], out[3:]


def local(grad_out, expert_ids, gate_probs, keep_mask, pre_gate, pre_up, w_down):
    dp = lax.axis_index("dp")
    expert = lax.axis_index("expert")
    etp = lax.axis_index("etp")
    x_lo, z = expert // 4, expert % 4
    x_hi, y = etp // 4, etp % 4
    x = x_hi * 2 + x_lo
    turned_y = (y - dp) % 4

    par_x = move(grad_out, near_pair)
    own_w = w_down[0]
    kept = gate_probs * keep_mask.astype(jnp.bfloat16)
    meta = jnp.concatenate(
        [
            expert_ids.T.astype(jnp.float32),
            kept.T.astype(jnp.float32),
            jnp.zeros((4, TOK), jnp.float32),
        ],
        axis=0,
    )
    par_meta = move(meta, near_pair)
    oth_w = move(own_w, other_core)

    sp = jnp.stack([z, x_lo, turned_y % 2]).astype(jnp.int32)
    sent = build_slots(sp, meta, par_meta, grad_out, par_x)
    slots = sent[4]
    arrived = {0: sent[0]}
    for k in (1, 3, 2):
        arrived[k] = move(sent[k], along_z(k))

    gate = pre_gate.reshape(2, 4, 2 * UNIT, FF)
    up = pre_up.reshape(2, 4, 2 * UNIT, FF)
    pair = turned_y // 2
    carried, sums = None, None
    order = (0, 1, 3, 2)
    for n, k in enumerate(order):
        same, other = arrived[k][:PAIR], arrived[k][PAIR:]
        own_y = jnp.concatenate(
            [
                same,
                move(other, along_x(1)),
                move(other, along_x(-1)),
                move(same, along_x(2)),
            ],
            axis=0,
        )
        par_y = move(own_y, far_pair)
        starts = []
        for p in (pair, 1 - pair):
            for away in (0, 3, 1, 2):
                source = (x + away) % 4
                starts.append(((source % 2) * 2 + source // 2) * UNIT + p * PAIR)
        sp = jnp.stack(
            [(z - k) % 4]
            + starts
            + [dp * CAP, (UNIT - dp * CAP) % UNIT, dp * HALF, (1 - dp) * HALF]
        ).astype(jnp.int32)
        carried, sums = run_chunk(
            n == 0, n == 3, sp, own_y, par_y, own_w, oth_w, gate, up, sums, carried
        )
    grad_gate, grad_up, term = carried
    grad_w = (sums[0] + move(sums[1], other_core).astype(jnp.float32)).astype(jnp.bfloat16)

    returned = lax.all_to_all(
        term.reshape(64, CAP), ("expert", "etp"), split_axis=0, concat_axis=0, tiled=True
    )
    summed = returned.reshape(EXPERTS, 8, CAP).sum(axis=1)
    hit = (expert_ids.T[:, :, None, None] == jnp.arange(EXPERTS)[None, None, :, None]) & (
        slots[:2, :, None, None] == jnp.arange(CAP, dtype=jnp.float32)[None, None, None, :]
    )
    picked = jnp.sum(jnp.where(hit, summed[None, None], 0.0), axis=(2, 3)).T
    kept_only = keep_mask.astype(jnp.float32) * picked
    grad_gate_probs = kept_only / gate_probs.astype(jnp.float32)
    return (
        grad_gate.reshape(1, ROWS, FF),
        grad_up.reshape(1, ROWS, FF),
        grad_w[None],
        grad_gate_probs,
    )


def solution(mesh):
    tokens = P(("dp", "expert", "etp"), None)
    acts = P("expert", "dp", "etp")
    weight = P("expert", "etp", "dp")
    return jax.shard_map(
        local,
        mesh=mesh,
        in_specs=(tokens, tokens, tokens, tokens, acts, acts, weight),
        out_specs=(acts, acts, weight, tokens),
        check_vma=False,
    )
```

time: 472 us -> 253 us (0.54); the launches traced: 466 us -> 253 us
  blocking collectives: 115 us -> 0 us
  waiting for transfers between devices: 170 us -> 69.5 us
  local copies, waits for them, and re-layouts: 100 us -> 8.86 us
  Pallas kernels: 0 us -> 90.4 us
  starting transfers between devices: 8.24 us -> 67.9 us
  matrix products: 40.8 us -> 0 us
  between operations: 14.8 us -> 0.82 us
    all_gather x2 -> x0, waiting for transfers between devices: 158 us -> none  [the longest x1 158 us: local(): lax.all_gather(arrived_grads, 'etp', axis=2, tiled=True)]
    pallas_call x0 -> x5, Pallas kernels: none -> 90.4 us  [the longest x4 85 us: run_chunk(): pl.pallas_call(functools.partial(chunk_kernel, first, last), grid_spec=pl...]
    ppermute x0 -> x23, waiting for transfers between devices: none -> 60 us  [move(): return lax.ppermute(array, AXES, pairs)]
    ppermute x0 -> x23, starting transfers between devices: none -> 48.5 us  [move(): return lax.ppermute(array, AXES, pairs)]
    unnamed x21 -> x20, local copies, waits for them, and re-layouts: 47.2 us -> 2.68 us
    all_to_all x3 -> x0, blocking collectives: 42.4 us -> none  [the longest x1 30 us: local(): lax.all_to_all(lax.all_to_all(send_grads.reshape(1, experts, capacity, mo...]
    dot_general x2 -> x0, matrix products: 40.8 us -> none  [the longest x1 21.6 us: contract_rows(): lax.dot_general(left, right, (((0,), (0,)), ((), ())), preferred_element_...]
    unnamed x1 -> x0, blocking collectives: 38.8 us -> none
  transfers between devices with their start and end apart: 5 -> 24, of which waited for: 3 -> 10; matrix products, arithmetic and copies ran while one was open for 2% -> 6% of each run, Pallas kernels for 0% -> 25%
where the time goes in v1:
time: 253 us
  Pallas kernels  90.4 us (36%)
  waiting for transfers between devices  69.5 us (27%)
  starting transfers between devices  67.9 us (27%)
  other arithmetic  15.5 us (6%)
  local copies, waits for them, and re-layouts  8.86 us (4%)
    pallas_call x4, Pallas kernels, run_chunk(): pl.pallas_call(functools.partial(chunk_kernel, first, last), grid_spec=pl...  85 us
    ppermute x23, waiting for transfers between devices, move(): return lax.ppermute(array, AXES, pairs)  60 us
    ppermute x23, starting transfers between devices, move(): return lax.ppermute(array, AXES, pairs)  48.5 us
    all_to_all x1, starting transfers between devices, local(): lax.all_to_all(term.reshape(64, CAP), ('expert', 'etp'), split_axis=0, co...  19.4 us
    all_to_all x1, waiting for transfers between devices, local(): lax.all_to_all(term.reshape(64, CAP), ('expert', 'etp'), split_axis=0, co...  9.5 us
    concatenate x4, other arithmetic, local(): jnp.concatenate([same, move(other, along_x(1)), move(other, along_x(-1)),...  5.51 us
    broadcast_in_dim x1, other arithmetic, local(): grad_w[None]  5.46 us
    pallas_call x1, Pallas kernels, build_slots(): pl.pallas_call(slots_kernel, grid_spec=pltpu.PrefetchScalarGridSpec(num_s...  5.42 us
  transfers between devices with their start and end apart: 24, of which 10 were waited for; matrix products, arithmetic and copies ran while one was open for 6% of the time, Pallas kernels for 25%

profile of v1, /device:TPU:0, one launch (start us, length us, event | category | flops | bytes accessed | tf_op | source)
XLA Modules:
  0.0 253.0 jit_solution(761025396251148334)
XLA Ops:
  0.6 1.7 collective-permute-start.1
  5.1 7.9 %collective-permute-done.par_meta = f32[8,128]{1,0:T(8,128)S(1)} collective-permute-done((f32[8,128]{1,0:T(8,128)S(1)}, f32[8,128]{1,0:T(8,128)S(1)}, u32[]{:S(2)}, u32[]{:S(2)}) %collective-permute-start) | collective-permute-done | bytes 4128 | tf_op jit(solution)/shard_map/ppermute | solution.py:41
  13.6 5.4 %shard_map.102 = (bf16[144,3072]{1,0:T(8,128)(2,1)}, bf16[144,3072]{1,0:T(8,128)(2,1)}, bf16[144,3072]{1,0:T(8,128)(2,1)}, bf16[144,3072]{1,0:T(8,128)(2,1)}, f32[8,128]{1,0:T(8,128)}) custom-call(s32[3]{0:T(128)} %pad_add_fusion.sp, f32[8,128]{1,0:T(8,128)} %copy-done.7, f32[8,128]{1,0:T(8,128)} %copy-done.9, bf16[128,3072]{1,0:T(8,128)(2,1)} %own_x.1, ...), custom_call_target="tpu_custom_call" | custom-call | flops 905969664 | bytes 6000000 | tf_op jit(solution)/shard_map/pallas_call | solution.py:120
  19.0 2.0 collective-permute-start.13
  22.3 1.6 collective-permute-start.18
  23.8 1.7 collective-permute-start.19
  25.6 1.8 collective-permute-start.20
  27.4 8.3 %collective-permute-done.18 = bf16[72,3072]{1,0:T(8,128)(2,1)S(1)} collective-permute-done((bf16[72,3072]{1,0:T(8,128)(2,1)S(1)}, bf16[72,3072]{1,0:T(8,128)(2,1)S(1)}, u32[]{:S(2)}, u32[]{:S(2)}) %collective-permute-start.18) | collective-permute-done | bytes 442400 | tf_op jit(solution)/shard_map/ppermute | solution.py:41
  35.6 2.1 collective-permute-start.8
  37.7 6.4 %collective-permute-done.19 = bf16[72,3072]{1,0:T(8,128)(2,1)S(1)} collective-permute-done((bf16[72,3072]{1,0:T(8,128)(2,1)S(1)}, bf16[72,3072]{1,0:T(8,128)(2,1)S(1)}, u32[]{:S(2)}, u32[]{:S(2)}) %collective-permute-start.19) | collective-permute-done | bytes 442400 | tf_op jit(solution)/shard_map/ppermute | solution.py:41
  44.1 1.7 collective-permute-done.20
  47.1 4.8 %collective-permute-start.21 = (bf16[288,3072]{1,0:T(8,128)(2,1)}, bf16[288,3072]{1,0:T(8,128)(2,1)}, u32[]{:S(2)}, u32[]{:S(2)}) collective-permute-start(bf16[288,3072]{1,0:T(8,128)(2,1)} %pad_maximum_fusion.3.refs_0_), channel_id=1, source_target_pairs={{0,3},{1,2},{2,1},{3,0},{4,7},{5,6},{6,5},{7,4},{8,11},{9,10},{10,... | collective-permute-start | bytes 5308424 | tf_op jit(solution)/shard_map/ppermute | solution.py:41
  52.1 23.1 %collective-permute-done.8 = bf16[144,3072]{1,0:T(8,128)(2,1)S(1)} collective-permute-done((bf16[144,3072]{1,0:T(8,128)(2,1)}, bf16[144,3072]{1,0:T(8,128)(2,1)S(1)}, u32[]{:S(2)}, u32[]{:S(2)}) %collective-permute-start.8) | collective-permute-done | bytes 884768 | tf_op jit(solution)/shard_map/ppermute | solution.py:41
  77.7 2.3 collective-permute-start.10
  80.0 3.7 %collective-permute-done.15 = bf16[72,3072]{1,0:T(8,128)(2,1)S(1)} collective-permute-done((bf16[72,3072]{1,0:T(8,128)(2,1)S(1)}, bf16[72,3072]{1,0:T(8,128)(2,1)S(1)}, u32[]{:S(2)}, u32[]{:S(2)}) %collective-permute-start.15) | collective-permute-done | bytes 442400 | tf_op jit(solution)/shard_map/ppermute | solution.py:41
  83.7 4.0 %collective-permute-start.11 = (bf16[72,3072]{1,0:T(8,128)(2,1)S(1)}, bf16[72,3072]{1,0:T(8,128)(2,1)S(1)}, u32[]{:S(2)}, u32[]{:S(2)}) collective-permute-start(bf16[72,3072]{1,0:T(8,128)(2,1)S(1)} %get-tuple-element.59), channel_id=1, source_target_pairs={{0,4},{1,5},{2,6},{3,7},{4,0},{5,1},{6,2},{7,3},{8,12},{9,13},{10,... | collective-permute-start | bytes 1327112 | tf_op jit(solution)/shard_map/ppermute | solution.py:41
  90.0 6.6 %collective-permute-start.9 = (bf16[72,3072]{1,0:T(8,128)(2,1)S(1)}, bf16[72,3072]{1,0:T(8,128)(2,1)S(1)}, u32[]{:S(2)}, u32[]{:S(2)}) collective-permute-start(bf16[72,3072]{1,0:T(8,128)(2,1)S(1)} %get-tuple-element.58), channel_id=1, source_target_pairs={{0,32},{1,33},{2,34},{3,35},{4,36},{5,37},{6,38},{7,39},{8,40},{9,... | collective-permute-start | bytes 1327112 | tf_op jit(solution)/shard_map/ppermute | solution.py:41
  96.6 4.7 %collective-permute-done.10 = bf16[72,3072]{1,0:T(8,128)(2,1)S(1)} collective-permute-done((bf16[72,3072]{1,0:T(8,128)(2,1)S(1)}, bf16[72,3072]{1,0:T(8,128)(2,1)S(1)}, u32[]{:S(2)}, u32[]{:S(2)}) %collective-permute-start.10) | collective-permute-done | bytes 442400 | tf_op jit(solution)/shard_map/ppermute | solution.py:41
  101.3 4.5 %collective-permute-start.3 = (bf16[72,3072]{1,0:T(8,128)(2,1)S(1)}, bf16[72,3072]{1,0:T(8,128)(2,1)S(1)}, u32[]{:S(2)}, u32[]{:S(2)}) collective-permute-start(bf16[72,3072]{1,0:T(8,128)(2,1)S(1)} %get-tuple-element.60), channel_id=1, source_target_pairs={{0,32},{1,33},{2,34},{3,35},{4,36},{5,37},{6,38},{7,39},{8,40},{9,... | collective-permute-start | bytes 1327112 | tf_op jit(solution)/shard_map/ppermute | solution.py:41
  107.2 2.8 %collective-permute-start.17 = (bf16[288,3072]{1,0:T(8,128)(2,1)}, bf16[288,3072]{1,0:T(8,128)(2,1)}, u32[]{:S(2)}, u32[]{:S(2)}) collective-permute-start(bf16[288,3072]{1,0:T(8,128)(2,1)} %pad_maximum_fusion.2.refs_0_), channel_id=1, source_target_pairs={{0,3},{1,2},{2,1},{3,0},{4,7},{5,6},{6,5},{7,4},{8,11},{9,10},{10,... | collective-permute-start | bytes 5308424 | tf_op jit(solution)/shard_map/ppermute | solution.py:41
  110.0 3.0 %collective-permute-start.4 = (bf16[72,3072]{1,0:T(8,128)(2,1)S(1)}, bf16[72,3072]{1,0:T(8,128)(2,1)S(1)}, u32[]{:S(2)}, u32[]{:S(2)}) collective-permute-start(bf16[72,3072]{1,0:T(8,128)(2,1)S(1)} %get-tuple-element.60), channel_id=1, source_target_pairs={{0,36},{1,37},{2,38},{3,39},{4,32},{5,33},{6,34},{7,35},{8,44},{9,... | collective-permute-start | bytes 1327112 | tf_op jit(solution)/shard_map/ppermute | solution.py:41
  113.0 2.6 %collective-permute-start.5 = (bf16[72,3072]{1,0:T(8,128)(2,1)}, bf16[72,3072]{1,0:T(8,128)(2,1)}, u32[]{:S(2)}, u32[]{:S(2)}) collective-permute-start(bf16[72,3072]{1,0:T(8,128)(2,1)} %get-tuple-element.61), channel_id=1, source_target_pairs={{0,4},{1,5},{2,6},{3,7},{4,0},{5,1},{6,2},{7,3},{8,12},{9,13},{10,... | collective-permute-start | bytes 1327112 | tf_op jit(solution)/shard_map/ppermute | solution.py:41
  117.0 2.9 %collective-permute-done.4 = bf16[72,3072]{1,0:T(8,128)(2,1)S(1)} collective-permute-done((bf16[72,3072]{1,0:T(8,128)(2,1)S(1)}, bf16[72,3072]{1,0:T(8,128)(2,1)S(1)}, u32[]{:S(2)}, u32[]{:S(2)}) %collective-permute-start.4) | collective-permute-done | bytes 442400 | tf_op jit(solution)/shard_map/ppermute | solution.py:41
  125.0 3.1 %collective-permute-start.6 = (bf16[288,3072]{1,0:T(8,128)(2,1)S(1)}, bf16[288,3072]{1,0:T(8,128)(2,1)S(1)}, u32[]{:S(2)}, u32[]{:S(2)}) collective-permute-start(bf16[288,3072]{1,0:T(8,128)(2,1)S(1)} %pad_maximum_fusion.refs_0_), channel_id=1, source_target_pairs={{0,3},{1,2},{2,1},{3,0},{4,7},{5,6},{6,5},{7,4},{8,11},{9,10},{10,... | collective-permute-start | bytes 5308424 | tf_op jit(solution)/shard_map/ppermute | solution.py:41
  128.2 20.6 %shard_map.103 = (bf16[2,4,288,1024]{3,2,1,0:T(8,128)(2,1)}, bf16[2,4,288,1024]{3,2,1,0:T(8,128)(2,1)}, f32[2,4,288,1]{3,2,1,0:T(8,128)}, f32[1024,1536]{1,0:T(8,128)}, f32[1024,1536]{1,0:T(8,128)}) custom-call(s32[13]{0:T(128)} %stack.131.sp, bf16[288,3072]{1,0:T(8,128)(2,1)} %pad_maximum_fusion.3.refs_0_, ...), custom_call_target="tpu_custom_call" | custom-call | flops 7247757312 | bytes 30000000 | tf_op jit(solution)/shard_map/pallas_call | solution.py:221
  148.7 21.5 %shard_map.104 = (bf16[2,4,288,1024]{3,2,1,0:T(8,128)(2,1)}, bf16[2,4,288,1024]{3,2,1,0:T(8,128)(2,1)}, f32[2,4,288,1]{3,2,1,0:T(8,128)}, f32[1024,1536]{1,0:T(8,128)}, f32[1024,1536]{1,0:T(8,128)}) custom-call(s32[13]{0:T(128)} %stack.129.sp, ...), custom_call_target="tpu_custom_call", output_to_operand_aliasing={{0}: (9, {}), {1}: (10, {}), {2}: (11, {})} | custom-call | flops 7247757312 | bytes 30000000 | tf_op jit(solution)/shard_map/pallas_call | solution.py:221
  170.3 21.6 %shard_map.105 = (bf16[2,4,288,1024]{3,2,1,0:T(8,128)(2,1)}, bf16[2,4,288,1024]{3,2,1,0:T(8,128)(2,1)}, f32[2,4,288,1]{3,2,1,0:T(8,128)}, f32[1024,1536]{1,0:T(8,128)}, f32[1024,1536]{1,0:T(8,128)}) custom-call(s32[13]{0:T(128)} %stack.127.sp, ...), custom_call_target="tpu_custom_call", output_to_operand_aliasing={{0}: (9, {}), {1}: (10, {}), {2}: (11, {})} | custom-call | flops 7247757312 | bytes 30000000 | tf_op jit(solution)/shard_map/pallas_call | solution.py:221
  193.2 21.3 %shard_map.106 = (bf16[2,4,288,1024]{3,2,1,0:T(8,128)(2,1)}, bf16[2,4,288,1024]{3,2,1,0:T(8,128)(2,1)}, f32[2,4,288,1]{3,2,1,0:T(8,128)}, f32[1024,1536]{1,0:T(8,128)}, bf16[1024,1536]{1,0:T(8,128)(2,1)}) custom-call(s32[13]{0:T(128)} %stack.121.sp, bf16[288,3072]{1,0:T(8,128)(2,1)} %copy-done.1, ...), custom_call_target="tpu_custom_call", output_to_operand_aliasing={{0}: (9, {}), {1}: (10, {}), {2}: (11, {})} | custom-call | flops 7247757312 | bytes 30000000 | tf_op jit(solution)/shard_map/pallas_call | solution.py:221
  215.3 1.7 reduce
  217.8 19.4 %all-to-all-start = ((f32[64,1,36]{2,1,0:T(1,128)}), f32[64,1,36]{2,1,0:T(1,128)S(1)}, u32[]{:S(2)}, u32[]{:S(2)}) async-start(f32[64,1,36]{2,1,0:T(1,128)} %bitcast.27), calls=%async_computation | async-start | bytes 65536 | tf_op jit(solution)/shard_map/all_to_all | solution.py:321
  237.2 9.5 %all-to-all-done = f32[64,1,36]{2,1,0:T(1,128)S(1)} async-done(((f32[64,1,36]{2,1,0:T(1,128)}), f32[64,1,36]{2,1,0:T(1,128)S(1)}, u32[]{:S(2)}, u32[]{:S(2)}) %all-to-all-start) | async-done | bytes 9248 | tf_op jit(solution)/shard_map/all_to_all | solution.py:321
  247.6 5.5 %fusion = bf16[1,1024,1536]{2,1,0:T(8,128)(2,1)} fusion(f32[1024,1536]{1,0:T(8,128)} %get-tuple-element.50, bf16[1024,1536]{1,0:T(8,128)(2,1)S(1)} %collective-permute-done.22), kind=kLoop, calls=%fused_computation.1 | loop fusion | flops 4718592 | bytes 12582912 | tf_op jit(solution)/shard_map/broadcast_in_dim | solution.py:334
  (69 shorter events, 22.1 us)
Async XLA Ops:
  0.6 26.7 %copy-start = (bf16[1,1024,1536]{2,1,0:T(8,128)(2,1)S(1)}, bf16[1,1024,1536]{2,1,0:T(8,128)(2,1)}, u32[]{:S(2)}) copy-start(bf16[1,1024,1536]{2,1,0:T(8,128)(2,1)} %param.13) | copy-start | bytes 9437188
  0.6 12.4 %collective-permute-start.1 = (bf16[128,3072]{1,0:T(8,128)(2,1)}, bf16[128,3072]{1,0:T(8,128)(2,1)}, u32[]{:S(2)}, u32[]{:S(2)}) collective-permute-start(bf16[128,3072]{1,0:T(8,128)(2,1)} %own_x.1), channel_id=1, source_target_pairs={{0,1},{1,0},{2,3},{3,2},{4,5},{5,4},{6,7},{7,6},{8,9},{9,8},{10,11... | collective-permute-start | bytes 2359304 | tf_op jit(solution)/shard_map/ppermute | solution.py:41
  3.9 9.1 %copy-start.7 = (f32[8,128]{1,0:T(8,128)}, f32[8,128]{1,0:T(8,128)S(1)}, u32[]{:S(2)}) copy-start(f32[8,128]{1,0:T(8,128)S(1)} %maximum_maximum_fusion.own_meta) | copy-start | bytes 12292
  3.9 9.1 %collective-permute-start = (f32[8,128]{1,0:T(8,128)S(1)}, f32[8,128]{1,0:T(8,128)S(1)}, u32[]{:S(2)}, u32[]{:S(2)}) collective-permute-start(f32[8,128]{1,0:T(8,128)S(1)} %maximum_maximum_fusion.own_meta), channel_id=1, source_target_pairs={{0,1},{1,0},{2,3},{3,2},{4,5},{5,4},{6,7},{7,6},{8,9},{9,8},{10,11... | collective-permute-start | bytes 12296 | tf_op jit(solution)/shard_map/ppermute | solution.py:41
  19.0 32.9 %collective-permute-start.13 = (bf16[144,3072]{1,0:T(8,128)(2,1)}, bf16[144,3072]{1,0:T(8,128)(2,1)S(1)}, u32[]{:S(2)}, u32[]{:S(2)}) collective-permute-start(bf16[144,3072]{1,0:T(8,128)(2,1)} %get-tuple-element.31), channel_id=1, source_target_pairs={{0,8},{1,9},{2,10},{3,11},{4,12},{5,13},{6,14},{7,15},{8,16},{9,17... | collective-permute-start | bytes 2654216 | tf_op jit(solution)/shard_map/ppermute | solution.py:41
  22.3 13.4 %collective-permute-start.18 = (bf16[72,3072]{1,0:T(8,128)(2,1)S(1)}, bf16[72,3072]{1,0:T(8,128)(2,1)S(1)}, u32[]{:S(2)}, u32[]{:S(2)}) collective-permute-start(bf16[72,3072]{1,0:T(8,128)(2,1)S(1)} %get-tuple-element.54), channel_id=1, source_target_pairs={{0,32},{1,33},{2,34},{3,35},{4,36},{5,37},{6,38},{7,39},{8,40},{9,... | collective-permute-start | bytes 1327112 | tf_op jit(solution)/shard_map/ppermute | solution.py:41
  23.8 20.3 %collective-permute-start.19 = (bf16[72,3072]{1,0:T(8,128)(2,1)S(1)}, bf16[72,3072]{1,0:T(8,128)(2,1)S(1)}, u32[]{:S(2)}, u32[]{:S(2)}) collective-permute-start(bf16[72,3072]{1,0:T(8,128)(2,1)S(1)} %get-tuple-element.54), channel_id=1, source_target_pairs={{0,36},{1,37},{2,38},{3,39},{4,32},{5,33},{6,34},{7,35},{8,44},{9,... | collective-permute-start | bytes 1327112 | tf_op jit(solution)/shard_map/ppermute | solution.py:41
  25.6 20.2 %collective-permute-start.20 = (bf16[72,3072]{1,0:T(8,128)(2,1)S(1)}, bf16[72,3072]{1,0:T(8,128)(2,1)S(1)}, u32[]{:S(2)}, u32[]{:S(2)}) collective-permute-start(bf16[72,3072]{1,0:T(8,128)(2,1)S(1)} %get-tuple-element.55), channel_id=1, source_target_pairs={{0,4},{1,5},{2,6},{3,7},{4,0},{5,1},{6,2},{7,3},{8,12},{9,13},{10,... | collective-permute-start | bytes 1327112 | tf_op jit(solution)/shard_map/ppermute | solution.py:41
  27.4 100.8 %collective-permute-start.7 = (bf16[1024,1536]{1,0:T(8,128)(2,1)S(1)}, bf16[1024,1536]{1,0:T(8,128)(2,1)}, u32[]{:S(2)}, u32[]{:S(2)}) collective-permute-start(bf16[1024,1536]{1,0:T(8,128)(2,1)S(1)} %bitcast.52), channel_id=1, source_target_pairs={{0,64},{1,65},{2,66},{3,67},{4,68},{5,69},{6,70},{7,71},{8,72},{9,... | collective-permute-start | bytes 9437192 | tf_op jit(solution)/shard_map/ppermute | solution.py:41
  35.6 39.5 %collective-permute-start.8 = (bf16[144,3072]{1,0:T(8,128)(2,1)}, bf16[144,3072]{1,0:T(8,128)(2,1)S(1)}, u32[]{:S(2)}, u32[]{:S(2)}) collective-permute-start(bf16[144,3072]{1,0:T(8,128)(2,1)} %get-tuple-element.30), channel_id=1, source_target_pairs={{0,24},{1,25},{2,26},{3,27},{4,28},{5,29},{6,30},{7,31},{8,0},{9,1... | collective-permute-start | bytes 2654216 | tf_op jit(solution)/shard_map/ppermute | solution.py:41
  44.1 32.7 %collective-permute-start.2 = (bf16[144,3072]{1,0:T(8,128)(2,1)}, bf16[144,3072]{1,0:T(8,128)(2,1)S(1)}, u32[]{:S(2)}, u32[]{:S(2)}) collective-permute-start(bf16[144,3072]{1,0:T(8,128)(2,1)} %get-tuple-element.29), channel_id=1, source_target_pairs={{0,16},{1,17},{2,18},{3,19},{4,20},{5,21},{6,22},{7,23},{8,24},{9,... | collective-permute-start | bytes 2654216 | tf_op jit(solution)/shard_map/ppermute | solution.py:41
  47.1 81.1 %collective-permute-start.21 = (bf16[288,3072]{1,0:T(8,128)(2,1)}, bf16[288,3072]{1,0:T(8,128)(2,1)}, u32[]{:S(2)}, u32[]{:S(2)}) collective-permute-start(bf16[288,3072]{1,0:T(8,128)(2,1)} %pad_maximum_fusion.3.refs_0_), channel_id=1, source_target_pairs={{0,3},{1,2},{2,1},{3,0},{4,7},{5,6},{6,5},{7,4},{8,11},{9,10},{10,... | collective-permute-start | bytes 5308424 | tf_op jit(solution)/shard_map/ppermute | solution.py:41
  52.0 25.7 %collective-permute-start.14 = (bf16[72,3072]{1,0:T(8,128)(2,1)S(1)}, bf16[72,3072]{1,0:T(8,128)(2,1)S(1)}, u32[]{:S(2)}, u32[]{:S(2)}) collective-permute-start(bf16[72,3072]{1,0:T(8,128)(2,1)S(1)} %get-tuple-element.56), channel_id=1, source_target_pairs={{0,32},{1,33},{2,34},{3,35},{4,36},{5,37},{6,38},{7,39},{8,40},{9,... | collective-permute-start | bytes 1327112 | tf_op jit(solution)/shard_map/ppermute | solution.py:41
  75.2 8.6 %collective-permute-start.15 = (bf16[72,3072]{1,0:T(8,128)(2,1)S(1)}, bf16[72,3072]{1,0:T(8,128)(2,1)S(1)}, u32[]{:S(2)}, u32[]{:S(2)}) collective-permute-start(bf16[72,3072]{1,0:T(8,128)(2,1)S(1)} %get-tuple-element.56), channel_id=1, source_target_pairs={{0,36},{1,37},{2,38},{3,39},{4,32},{5,33},{6,34},{7,35},{8,44},{9,... | collective-permute-start | bytes 1327112 | tf_op jit(solution)/shard_map/ppermute | solution.py:41
  76.8 13.2 %collective-permute-start.16 = (bf16[72,3072]{1,0:T(8,128)(2,1)S(1)}, bf16[72,3072]{1,0:T(8,128)(2,1)S(1)}, u32[]{:S(2)}, u32[]{:S(2)}) collective-permute-start(bf16[72,3072]{1,0:T(8,128)(2,1)S(1)} %get-tuple-element.57), channel_id=1, source_target_pairs={{0,4},{1,5},{2,6},{3,7},{4,0},{5,1},{6,2},{7,3},{8,12},{9,13},{10,... | collective-permute-start | bytes 1327112 | tf_op jit(solution)/shard_map/ppermute | solution.py:41
  77.7 23.6 %collective-permute-start.10 = (bf16[72,3072]{1,0:T(8,128)(2,1)S(1)}, bf16[72,3072]{1,0:T(8,128)(2,1)S(1)}, u32[]{:S(2)}, u32[]{:S(2)}) collective-permute-start(bf16[72,3072]{1,0:T(8,128)(2,1)S(1)} %get-tuple-element.58), channel_id=1, source_target_pairs={{0,36},{1,37},{2,38},{3,39},{4,32},{5,33},{6,34},{7,35},{8,44},{9,... | collective-permute-start | bytes 1327112 | tf_op jit(solution)/shard_map/ppermute | solution.py:41
  83.7 23.4 %collective-permute-start.11 = (bf16[72,3072]{1,0:T(8,128)(2,1)S(1)}, bf16[72,3072]{1,0:T(8,128)(2,1)S(1)}, u32[]{:S(2)}, u32[]{:S(2)}) collective-permute-start(bf16[72,3072]{1,0:T(8,128)(2,1)S(1)} %get-tuple-element.59), channel_id=1, source_target_pairs={{0,4},{1,5},{2,6},{3,7},{4,0},{5,1},{6,2},{7,3},{8,12},{9,13},{10,... | collective-permute-start | bytes 1327112 | tf_op jit(solution)/shard_map/ppermute | solution.py:41
  90.0 20.0 %collective-permute-start.9 = (bf16[72,3072]{1,0:T(8,128)(2,1)S(1)}, bf16[72,3072]{1,0:T(8,128)(2,1)S(1)}, u32[]{:S(2)}, u32[]{:S(2)}) collective-permute-start(bf16[72,3072]{1,0:T(8,128)(2,1)S(1)} %get-tuple-element.58), channel_id=1, source_target_pairs={{0,32},{1,33},{2,34},{3,35},{4,36},{5,37},{6,38},{7,39},{8,40},{9,... | collective-permute-start | bytes 1327112 | tf_op jit(solution)/shard_map/ppermute | solution.py:41
  101.3 11.7 %collective-permute-start.3 = (bf16[72,3072]{1,0:T(8,128)(2,1)S(1)}, bf16[72,3072]{1,0:T(8,128)(2,1)S(1)}, u32[]{:S(2)}, u32[]{:S(2)}) collective-permute-start(bf16[72,3072]{1,0:T(8,128)(2,1)S(1)} %get-tuple-element.60), channel_id=1, source_target_pairs={{0,32},{1,33},{2,34},{3,35},{4,36},{5,37},{6,38},{7,39},{8,40},{9,... | collective-permute-start | bytes 1327112 | tf_op jit(solution)/shard_map/ppermute | solution.py:41
  107.2 41.6 %collective-permute-start.17 = (bf16[288,3072]{1,0:T(8,128)(2,1)}, bf16[288,3072]{1,0:T(8,128)(2,1)}, u32[]{:S(2)}, u32[]{:S(2)}) collective-permute-start(bf16[288,3072]{1,0:T(8,128)(2,1)} %pad_maximum_fusion.2.refs_0_), channel_id=1, source_target_pairs={{0,3},{1,2},{2,1},{3,0},{4,7},{5,6},{6,5},{7,4},{8,11},{9,10},{10,... | collective-permute-start | bytes 5308424 | tf_op jit(solution)/shard_map/ppermute | solution.py:41
  110.0 9.9 %collective-permute-start.4 = (bf16[72,3072]{1,0:T(8,128)(2,1)S(1)}, bf16[72,3072]{1,0:T(8,128)(2,1)S(1)}, u32[]{:S(2)}, u32[]{:S(2)}) collective-permute-start(bf16[72,3072]{1,0:T(8,128)(2,1)S(1)} %get-tuple-element.60), channel_id=1, source_target_pairs={{0,36},{1,37},{2,38},{3,39},{4,32},{5,33},{6,34},{7,35},{8,44},{9,... | collective-permute-start | bytes 1327112 | tf_op jit(solution)/shard_map/ppermute | solution.py:41
  113.0 6.8 %copy-start.3 = (bf16[72,3072]{1,0:T(8,128)(2,1)}, bf16[72,3072]{1,0:T(8,128)(2,1)S(1)}, u32[]{:S(2)}) copy-start(bf16[72,3072]{1,0:T(8,128)(2,1)S(1)} %collective-permute-done.3) | copy-start | bytes 1327108
  113.0 10.4 %collective-permute-start.5 = (bf16[72,3072]{1,0:T(8,128)(2,1)}, bf16[72,3072]{1,0:T(8,128)(2,1)}, u32[]{:S(2)}, u32[]{:S(2)}) collective-permute-start(bf16[72,3072]{1,0:T(8,128)(2,1)} %get-tuple-element.61), channel_id=1, source_target_pairs={{0,4},{1,5},{2,6},{3,7},{4,0},{5,1},{6,2},{7,3},{8,12},{9,13},{10,... | collective-permute-start | bytes 1327112 | tf_op jit(solution)/shard_map/ppermute | solution.py:41
  120.6 49.7 %collective-permute-start.12 = (bf16[288,3072]{1,0:T(8,128)(2,1)}, bf16[288,3072]{1,0:T(8,128)(2,1)}, u32[]{:S(2)}, u32[]{:S(2)}) collective-permute-start(bf16[288,3072]{1,0:T(8,128)(2,1)} %pad_maximum_fusion.1.refs_0_), channel_id=1, source_target_pairs={{0,3},{1,2},{2,1},{3,0},{4,7},{5,6},{6,5},{7,4},{8,11},{9,10},{10,... | collective-permute-start | bytes 5308424 | tf_op jit(solution)/shard_map/ppermute | solution.py:41
  125.0 23.7 %copy-start.1 = (bf16[288,3072]{1,0:T(8,128)(2,1)}, bf16[288,3072]{1,0:T(8,128)(2,1)S(1)}, u32[]{:S(2)}) copy-start(bf16[288,3072]{1,0:T(8,128)(2,1)S(1)} %pad_maximum_fusion.refs_0_) | copy-start | bytes 5308420
  125.0 66.8 %collective-permute-start.6 = (bf16[288,3072]{1,0:T(8,128)(2,1)S(1)}, bf16[288,3072]{1,0:T(8,128)(2,1)S(1)}, u32[]{:S(2)}, u32[]{:S(2)}) collective-permute-start(bf16[288,3072]{1,0:T(8,128)(2,1)S(1)} %pad_maximum_fusion.refs_0_), channel_id=1, source_target_pairs={{0,3},{1,2},{2,1},{3,0},{4,7},{5,6},{6,5},{7,4},{8,11},{9,10},{10,... | collective-permute-start | bytes 5308424 | tf_op jit(solution)/shard_map/ppermute | solution.py:41
  191.9 1.3 copy-start.2
  193.2 21.5 %copy-start.5 = (s32[128,2]{0,1:T(2,128)S(1)}, s32[128,2]{0,1:T(2,128)}, u32[]{:S(2)}) copy-start(s32[128,2]{0,1:T(2,128)} %param.8) | copy-start | bytes 3076
  193.2 53.8 %copy-start.6 = (s32[128,2]{0,1:T(2,128)S(1)}, s32[128,2]{0,1:T(2,128)}, u32[]{:S(2)}) copy-start(s32[128,2]{0,1:T(2,128)} %param.10) | copy-start | bytes 3076
  193.2 53.8 %copy-start.8 = (bf16[128,2]{0,1:T(2,128)(2,1)S(1)}, bf16[128,2]{0,1:T(2,128)(2,1)}, u32[]{:S(2)}) copy-start(bf16[128,2]{0,1:T(2,128)(2,1)} %param.9) | copy-start | bytes 1540
  214.5 33.0 %collective-permute-start.22 = (bf16[1024,1536]{1,0:T(8,128)(2,1)}, bf16[1024,1536]{1,0:T(8,128)(2,1)S(1)}, u32[]{:S(2)}, u32[]{:S(2)}) collective-permute-start(bf16[1024,1536]{1,0:T(8,128)(2,1)} %get-tuple-element.51), channel_id=1, source_target_pairs={{0,64},{1,65},{2,66},{3,67},{4,68},{5,69},{6,70},{7,71},{8,72},{9,... | collective-permute-start | bytes 9437192 | tf_op jit(solution)/shard_map/ppermute | solution.py:41
  217.8 28.9 %all-to-all-start = ((f32[64,1,36]{2,1,0:T(1,128)}), f32[64,1,36]{2,1,0:T(1,128)S(1)}, u32[]{:S(2)}, u32[]{:S(2)}) async-start(f32[64,1,36]{2,1,0:T(1,128)} %bitcast.27), calls=%async_computation | async-start | bytes 65536 | tf_op jit(solution)/shard_map/all_to_all | solution.py:321
  (2 other events, 1.4 us)
